TPU v7x, 32 devices: a whole 2x2x4 slice. The times are simulated.
32 devices in a mesh: groups: 2 (over y), blk: 4 (over z), width: 4 (over x, core).
Axes of the slice: x: 2, y: 2, z: 4, core: 2. Of those that a mesh axis runs over, the one named last changes fastest.
Arguments:
- t_query: bfloat16 [128, 4096], P(('groups', 'blk'), 'width'), parts along dimension 0
- t_pass: bfloat16 [16384, 4096], P(('groups', 'blk'), 'width'), parts along dimension 0
- s_query: bfloat16 [128, 768], P(('groups', 'blk')), parts along dimension 0
- s_pass: bfloat16 [16384, 768], P(('groups', 'blk', 'width')), parts along dimension 0
- positive: int32 [128], P('groups'), parts along dimension 0, may hold values from 0 to 8191
- doc_ids: int32 [16384], P('groups'), parts along dimension 0, may hold values from 0 to 2047, never falling along the last dimension, each value on 1 to 8 neighbouring positions
Outputs:
- grad_query: float32 [128, 768], P(('groups', 'blk')), parts along dimension 0
- grad_passage: float32 [16384, 768], P(('groups', 'blk', 'width')), parts along dimension 0
There are 2 independent parts, one for each index of `groups`. A program takes and returns all parts, laid end to end along the dimension named above; each array names one. Nothing has to cross between parts.
Inputs may be any that keep to these rules, and one draw needn't show every extreme that they name: `doc_ids`: ids never fall along the passages; at most 8 passages share one.
All inputs are finite; a program needn't handle non-finite values.
Results may differ from a plain program's by a relative error of at most 0.0022.
Values may be sent and summed in bfloat16 or wider, within the bound.
A program may use at most 64 MiB of HBM per device.

v0:
```python
import math

import jax
import jax.numpy as jnp
from jax import lax
from jax.sharding import PartitionSpec as P

T_WIDTH = 4096
S_WIDTH = 768


TEMPER = 2.0
MASK_FILL = -1e30


def shifted(block, axis, distance):
    devices = range(lax.axis_size(axis))
    route = [((i - distance) % len(devices), i) for i in devices]
    return lax.ppermute(block, axis, route)


def joined(x, axis, combine):
    everything = jax.tree.map(lambda part: lax.all_gather(part, axis), x)
    leading = jax.tree.map(lambda part: part[0], everything)

    def lap(k, so_far):
        return combine(so_far, jax.tree.map(lambda part: part[k], everything))

    return lax.fori_loop(1, lax.axis_size(axis), lap, leading)


def combine_totals(first, second):
    merged = []
    for place in (0, 2):
        highest = jnp.maximum(first[place], second[place])
        summed = first[place + 1] * jnp.exp(first[place] - highest) + second[place + 1] * jnp.exp(
            second[place] - highest
        )
        merged.append(highest)
        merged.append(summed)
    return tuple(merged)


def row_totals(scores, masked):
    filled = jnp.where(masked, MASK_FILL, scores)
    highest = jnp.max(filled, axis=1)
    summed = jnp.sum(jnp.exp(filled - highest[:, None]), axis=1)
    return (highest, summed, filled)


def body(t_query, t_pass, s_query, s_pass, positive, doc_ids):
    panel_rows = s_query.shape[0]
    blocks = lax.axis_size("blk")
    widths = lax.axis_size("width")
    total_queries = positive.shape[0]
    own_rows = s_pass.shape[0]
    home = lax.axis_index("blk")
    first_row = (home * widths + lax.axis_index("width")) * own_rows
    t_scale = TEMPER / math.sqrt(T_WIDTH)
    s_scale = TEMPER / math.sqrt(S_WIDTH)
    local_docs = lax.dynamic_slice_in_dim(doc_ids, first_row, own_rows)
    target_docs = jnp.take(doc_ids, positive)
    columns = first_row + jnp.arange(own_rows, dtype=jnp.int32)
    is_positive = columns[None, :] == positive[:, None]
    masked = (local_docs[None, :] == target_docs[:, None]) & jnp.logical_not(is_positive)
    t_rows = lax.all_to_all(t_pass, "width", split_axis=0, concat_axis=1, tiled=True)
    whole_panel = lax.all_gather(t_query, "width", axis=1, tiled=True)

    def teacher_scores(panel):
        return jnp.einsum("qd,pd->qp", panel, t_rows, preferred_element_type=jnp.float32)

    def pass_on(panels):
        return shifted((panels[0], panels[1]), "blk", 1)

    panels = (whole_panel, s_query)

    def record(step, panels, stores):
        owner = (home - step) % blocks
        start = owner * panel_rows
        teach = teacher_scores(panels[0]) * t_scale
        learn = (
            jnp.einsum("qd,pd->qp", panels[1], s_pass, preferred_element_type=jnp.float32) * s_scale
        )
        return (
            lax.dynamic_update_slice_in_dim(stores[0], teach, start, 0),
            lax.dynamic_update_slice_in_dim(stores[1], learn, start, 0),
            lax.dynamic_update_slice_in_dim(stores[2], panels[1], start, 0),
        )

    def turn(step, carry):
        moving, stores = carry
        stores = record(step, moving, stores)
        return (pass_on(moving), stores)

    stores = (
        jnp.zeros((total_queries, own_rows), jnp.float32),
        jnp.zeros((total_queries, own_rows), jnp.float32),
        jnp.zeros((total_queries, s_query.shape[1]), jnp.bfloat16),
    )
    panels, stores = lax.fori_loop(0, blocks - 1, turn, (panels, stores))
    teach_all, learn_all, queries_all = record(blocks - 1, panels, stores)
    teach_high, teach_sum, teach_fill = row_totals(teach_all, masked)
    learn_high, learn_sum, learn_fill = row_totals(learn_all, masked)
    merged = joined(
        (teach_high, teach_sum, learn_high, learn_sum), ("blk", "width"), combine_totals
    )
    teach_log = merged[0] + jnp.log(merged[1])
    learn_log = merged[2] + jnp.log(merged[3])
    teach_probs = jnp.exp(teach_fill - teach_log[:, None])
    learn_probs = jnp.exp(learn_fill - learn_log[:, None])
    slope = (2.0 * learn_probs - teach_probs - is_positive.astype(jnp.float32)).astype(jnp.bfloat16)
    grad_passage = (
        jnp.einsum("qp,qd->pd", slope, queries_all, preferred_element_type=jnp.float32) * s_scale
    )

    def visit(step, carried_sum):
        owner = (home - step) % blocks
        slope_rows = lax.dynamic_slice_in_dim(slope, owner * panel_rows, panel_rows, 0)
        carried_sum = (
            carried_sum + jnp.dot(slope_rows, s_pass, preferred_element_type=jnp.float32) * s_scale
        )
        return shifted(carried_sum, "blk", 1)

    width_part = lax.fori_loop(
        0, blocks, visit, jnp.zeros((panel_rows, s_pass.shape[1]), jnp.float32)
    )
    grad_query = lax.psum(width_part, "width")
    return (grad_query, grad_passage)


def solution(mesh):
    placed = (
        P(("groups", "blk"), "width"),
        P(("groups", "blk"), "width"),
        P(("groups", "blk"), None),
        P(("groups", "blk", "width"), None),
        P("groups"),
        P("groups"),
    )
    return jax.shard_map(
        body,
        mesh=mesh,
        in_specs=placed,
        out_specs=(P(("groups", "blk"), None), P(("groups", "blk", "width"), None)),
        check_vma=False,
    )
```

profile of v0, /device:TPU:0, one launch (start us, length us, event | category | flops | bytes accessed | tf_op | source)
XLA Modules:
  0.0 193.0 jit_solution(3950361209150964265)
XLA Ops:
  0.6 0.0 copy-start.1
  0.6 0.0 copy-start.4
  0.7 0.0 copy-start.5
  0.7 0.0 copy-start.3
  0.7 5.0 %all-to-all-start = ((bf16[4,512,1024]{2,1,0:T(8,128)(2,1)}), bf16[4,512,1024]{2,1,0:T(8,128)(2,1)}, u32[]{:S(2)}, u32[]{:S(2)}) async-start(bf16[4,512,1024]{2,1,0:T(8,128)(2,1)} %bitcast.56), calls=%async_computation | async-start | bytes 8388608 | tf_op jit(solution)/shard_map/all_to_all | solution.py:66
  5.7 0.0 copy-done.1
  5.7 0.1 dynamic_slice.53
  5.8 0.0 copy-done.4
  5.8 0.8 gather_fusion
  6.6 0.0 copy-done.5
  6.6 0.7 dynamic-slice
  7.9 48.0 %all_gather.27 = bf16[16,4096]{1,0:T(8,128)(2,1)S(1)} all-gather(bf16[16,1024]{1,0:T(8,128)(2,1)S(1)} %copy-done.3), channel_id=1, replica_groups=mesh['groups'=2,'blk'=4,'width'=4] {'width'}, dimensions={1}, use_global_device_ids=true | all-gather | bytes 163840 | tf_op jit(solution)/shard_map/all_gather | solution.py:67
  55.9 0.0 all-to-all-done
  56.0 6.2 %copy.10 = bf16[4,512,1024]{1,2,0:T(8,128)(2,1)} copy(bf16[4,512,1024]{2,1,0:T(8,128)(2,1)} %all-to-all-done) | data formatting | bytes 8388608 | tf_op jit(solution)/shard_map/all_to_all | solution.py:66
  62.2 6.5 %copy.11 = bf16[512,4096]{1,0:T(8,128)(2,1)} copy(bf16[512,4096]{0,1:T(8,128)(2,1)} %bitcast.54) | data formatting | bytes 8388608 | tf_op jit(solution)/shard_map/while | solution.py:100
  68.7 23.9 %while.59 = (s32[]{:T(128)}, bf16[16,4096]{1,0:T(8,128)(2,1)S(1)}, bf16[16,768]{1,0:T(8,128)(2,1)S(1)}, f32[64,512]{1,0:T(8,128)S(1)}, f32[64,512]{1,0:T(8,128)S...) while((s32[]{:T(128)}, bf16[16,4096]{1,0:T(8,128)(2,1)S(1)}, ...), condition=%wide.region_1.2_spmd, body=%wide.region_0.1_spmd.sunk | while | flops 79708176 | bytes 6185360 | solution.py:100
  68.7 2.5 %collective-permute-start.1 = (bf16[16,768]{1,0:T(8,128)(2,1)S(1)}, bf16[16,768]{1,0:T(8,128)(2,1)S(1)}, u32[]{:S(2)}, u32[]{:S(2)}) collective-permute-start(bf16[16,768]{1,0:T(8,128)(2,1)S(1)} %copy.23), channel_id=1, source_target_pairs={{12,0},{0,4},{4,8},{8,12},{13,1},{1,5},{5,9},{9,13},{14,2},{2,6},{... | collective-permute-start | bytes 73736 | tf_op jit(solution)/shard_map/while/body/eval_jaxpr/ppermute | solution.py:19
  71.2 1.6 collective-permute-start
  72.8 3.4 %fusion.51 = f32[64,512]{1,0:T(8,128)S(1)} fusion(f32[64,512]{1,0:T(8,128)S(1)} %get-tuple-element.831, s32[]{:T(128)S(6)} %select_n.133, bf16[16,4096]{1,0:T(8,128)(2,1)S(1)} %copy.22, bf16[512,4096]{1,0:T(8,128)(2,1)} %get-tuple-element.849), kind=kOutput, calls=%fused_computation.4.clone.1 | convolution fusion | flops 67117056 | bytes 4358148 | tf_op jit(solution)/shard_map/while/body/eval_jaxpr/qd,pd->qp/dot_general | solution.py:70
  76.2 0.3 fusion.52
  76.5 0.0 collective-permute-done.1
  76.5 2.0 %collective-permute-done = bf16[16,4096]{1,0:T(8,128)(2,1)S(1)} collective-permute-done((bf16[16,4096]{1,0:T(8,128)(2,1)S(1)}, bf16[16,4096]{1,0:T(8,128)(2,1)S(1)}, u32[]{:S(2)}, u32[]{:S(2)}) %collective-permute-start) | collective-permute-done | bytes 131104 | tf_op jit(solution)/shard_map/while/body/eval_jaxpr/ppermute | solution.py:19
  78.5 0.0 collective-permute-start.1
  78.5 1.4 collective-permute-start
  79.9 3.4 %fusion.51 = f32[64,512]{1,0:T(8,128)S(1)} fusion(f32[64,512]{1,0:T(8,128)S(1)} %get-tuple-element.831, s32[]{:T(128)S(6)} %select_n.133, bf16[16,4096]{1,0:T(8,128)(2,1)S(1)} %copy.22, bf16[512,4096]{1,0:T(8,128)(2,1)} %get-tuple-element.849), kind=kOutput, calls=%fused_computation.4.clone.1 | convolution fusion | flops 67117056 | bytes 4358148 | tf_op jit(solution)/shard_map/while/body/eval_jaxpr/qd,pd->qp/dot_general | solution.py:70
  83.3 0.3 fusion.52
  83.6 0.5 collective-permute-done.1
  84.1 1.4 collective-permute-done
  85.5 0.0 collective-permute-start.1
  85.5 1.8 collective-permute-start
  87.4 3.4 %fusion.51 = f32[64,512]{1,0:T(8,128)S(1)} fusion(f32[64,512]{1,0:T(8,128)S(1)} %get-tuple-element.831, s32[]{:T(128)S(6)} %select_n.133, bf16[16,4096]{1,0:T(8,128)(2,1)S(1)} %copy.22, bf16[512,4096]{1,0:T(8,128)(2,1)} %get-tuple-element.849), kind=kOutput, calls=%fused_computation.4.clone.1 | convolution fusion | flops 67117056 | bytes 4358148 | tf_op jit(solution)/shard_map/while/body/eval_jaxpr/qd,pd->qp/dot_general | solution.py:70
  90.8 0.3 fusion.52
  91.1 0.1 collective-permute-done.1
  91.2 1.4 collective-permute-done
  92.6 2.8 %fusion.16 = f32[64,512]{1,0:T(8,128)S(1)} fusion(f32[64,512]{1,0:T(8,128)S(1)} %get-tuple-element.585, s32[]{:T(128)S(6)} %select_n.106, bf16[16,4096]{1,0:T(8,128)(2,1)S(1)} %get-tuple-element.586, bf16[512,4096]{0,1:T(8,128)(2,1)} %bitcast.55), kind=kOutput, calls=%fused_computation.28 | convolution fusion | flops 67117056 | bytes 4358148 | tf_op jit(solution)/shard_map/qd,pd->qp/dot_general | solution.py:70
  95.4 0.3 fusion.15
  95.7 0.2 fusion.22
  95.9 0.2 exponential_reduce_fusion
  96.2 0.2 dynamic-update-slice.2
  96.4 0.2 dynamic-update-slice
  96.7 0.2 dynamic-update-slice.3
  96.9 0.2 dynamic-update-slice.1
  97.1 57.6 %all-reduce.4 = (f32[1024]{0:T(1024)S(1)}, f32[1024]{0:T(1024)S(1)}, f32[1024]{0:T(1024)S(1)}, f32[1024]{0:T(1024)S(1)}) all-reduce(f32[1024]{0:T(1024)S(1)} %dynamic-update-slice, f32[1024]{0:T(1024)S(1)} %dynamic-update-slice.1, f32[1024]{0:T(1024)S(1)} %dynamic-update-slice.2, ...), channel_id=2, replica_groups=mesh['groups'=2,'blk'=4,'width'=4] {'blk','width'}, use_global_device_ids=true, to_apply=%add | all-reduce | flops 4096 | bytes 32768
  154.7 0.1 reshape.32
  154.8 0.1 reshape.33
  154.9 0.1 reshape.34
  154.9 0.1 reshape.35
  155.0 0.7 while.60
  155.8 0.2 fusion.18
  155.9 1.5 convolution_multiply_fusion.3
  157.5 24.4 %while.61 = (s32[]{:T(128)}, f32[16,768]{1,0:T(8,128)S(1)}, s32[]{:T(128)}, bf16[64,512]{1,0:T(8,128)(2,1)S(1)}, bf16[512,768]{1,0:T(8,128)(2,1)S(1)}, /*index=5...) while((s32[]{:T(128)}, f32[16,768]{1,0:T(8,128)S(1)}, s32[]{:T(128)}, ...), condition=%wide.region_9.10_spmd, body=%wide.region_8.9_spmd.sunk | while | flops 12607506 | bytes 1098048 | solution.py:124
  157.5 0.2 fusion.56
  157.7 0.0 collective-permute-start.2
  157.7 5.9 %collective-permute-done.2 = f32[16,768]{1,0:T(8,128)S(1)} collective-permute-done((f32[16,768]{1,0:T(8,128)S(1)}, f32[16,768]{1,0:T(8,128)S(1)}, u32[]{:S(2)}, u32[]{:S(2)}) %collective-permute-start.2) | collective-permute-done | bytes 49184 | tf_op jit(solution)/shard_map/while/body/eval_jaxpr/ppermute | solution.py:19
  163.6 0.2 fusion.56
  163.8 0.0 collective-permute-start.2
  163.8 5.9 %collective-permute-done.2 = f32[16,768]{1,0:T(8,128)S(1)} collective-permute-done((f32[16,768]{1,0:T(8,128)S(1)}, f32[16,768]{1,0:T(8,128)S(1)}, u32[]{:S(2)}, u32[]{:S(2)}) %collective-permute-start.2) | collective-permute-done | bytes 49184 | tf_op jit(solution)/shard_map/while/body/eval_jaxpr/ppermute | solution.py:19
  169.7 0.2 fusion.56
  169.9 0.0 collective-permute-start.2
  169.9 5.9 %collective-permute-done.2 = f32[16,768]{1,0:T(8,128)S(1)} collective-permute-done((f32[16,768]{1,0:T(8,128)S(1)}, f32[16,768]{1,0:T(8,128)S(1)}, u32[]{:S(2)}, u32[]{:S(2)}) %collective-permute-start.2) | collective-permute-done | bytes 49184 | tf_op jit(solution)/shard_map/while/body/eval_jaxpr/ppermute | solution.py:19
  175.8 0.2 fusion.56
  176.0 0.0 collective-permute-start.2
  176.0 5.9 %collective-permute-done.2 = f32[16,768]{1,0:T(8,128)S(1)} collective-permute-done((f32[16,768]{1,0:T(8,128)S(1)}, f32[16,768]{1,0:T(8,128)S(1)}, u32[]{:S(2)}, u32[]{:S(2)}) %collective-permute-start.2) | collective-permute-done | bytes 49184 | tf_op jit(solution)/shard_map/while/body/eval_jaxpr/ppermute | solution.py:19
  181.9 11.1 %psum.7 = f32[16,768]{1,0:T(8,128)} all-reduce(f32[16,768]{1,0:T(8,128)S(1)} %get-tuple-element.591), channel_id=1, replica_groups=mesh['groups'=2,'blk'=4,'width'=4] {'width'}, use_global_device_ids=true, to_apply=%region_10.11 | all-reduce | flops 12288 | bytes 98304 | tf_op jit(solution)/shard_map/psum | solution.py:127
  (47 shorter events, 0.6 us)
Async XLA Ops:
  0.6 5.1 %copy-start.1 = (s32[8192]{0:T(1024)S(1)}, s32[8192]{0:T(1024)}, u32[]{:S(2)}) copy-start(s32[8192]{0:T(1024)} %param.17) | copy-start | bytes 98308
  0.6 5.1 %copy-start.4 = (s32[64]{0:T(128)S(1)}, s32[64]{0:T(128)}, u32[]{:S(2)}) copy-start(s32[64]{0:T(128)} %param.16) | copy-start | bytes 772
  0.7 5.9 %copy-start.5 = (u32[32]{0:T(128)S(1)}, u32[32]{0:T(128)}, u32[]{:S(2)}) copy-start(u32[32]{0:T(128)} %constant.246) | copy-start | bytes 388
  0.7 7.3 %copy-start.3 = (bf16[16,1024]{1,0:T(8,128)(2,1)S(1)}, bf16[16,1024]{1,0:T(8,128)(2,1)}, u32[]{:S(2)}) copy-start(bf16[16,1024]{1,0:T(8,128)(2,1)} %param.12) | copy-start | bytes 98308
  0.7 55.3 %all-to-all-start = ((bf16[4,512,1024]{2,1,0:T(8,128)(2,1)}), bf16[4,512,1024]{2,1,0:T(8,128)(2,1)}, u32[]{:S(2)}, u32[]{:S(2)}) async-start(bf16[4,512,1024]{2,1,0:T(8,128)(2,1)} %bitcast.56), calls=%async_computation | async-start | bytes 8388608 | tf_op jit(solution)/shard_map/all_to_all | solution.py:66
  62.2 6.5 %copy-start = (bf16[512,768]{1,0:T(8,128)(2,1)S(1)}, bf16[512,768]{1,0:T(8,128)(2,1)}, u32[]{:S(2)}) copy-start(bf16[512,768]{1,0:T(8,128)(2,1)} %param.15) | copy-start | bytes 2359300
  62.2 6.5 %copy-start.2 = (bf16[16,768]{1,0:T(8,128)(2,1)S(1)}, bf16[16,768]{1,0:T(8,128)(2,1)}, u32[]{:S(2)}) copy-start(bf16[16,768]{1,0:T(8,128)(2,1)} %param.14) | copy-start | bytes 73732
  68.7 7.8 %collective-permute-start.1 = (bf16[16,768]{1,0:T(8,128)(2,1)S(1)}, bf16[16,768]{1,0:T(8,128)(2,1)S(1)}, u32[]{:S(2)}, u32[]{:S(2)}) collective-permute-start(bf16[16,768]{1,0:T(8,128)(2,1)S(1)} %copy.23), channel_id=1, source_target_pairs={{12,0},{0,4},{4,8},{8,12},{13,1},{1,5},{5,9},{9,13},{14,2},{2,6},{... | collective-permute-start | bytes 73736 | tf_op jit(solution)/shard_map/while/body/eval_jaxpr/ppermute | solution.py:19
  71.2 7.3 %collective-permute-start = (bf16[16,4096]{1,0:T(8,128)(2,1)S(1)}, bf16[16,4096]{1,0:T(8,128)(2,1)S(1)}, u32[]{:S(2)}, u32[]{:S(2)}) collective-permute-start(bf16[16,4096]{1,0:T(8,128)(2,1)S(1)} %copy.22), channel_id=1, source_target_pairs={{12,0},{0,4},{4,8},{8,12},{13,1},{1,5},{5,9},{9,13},{14,2},{2,6},{... | collective-permute-start | bytes 393224 | tf_op jit(solution)/shard_map/while/body/eval_jaxpr/ppermute | solution.py:19
  78.5 5.6 %collective-permute-start.1 = (bf16[16,768]{1,0:T(8,128)(2,1)S(1)}, bf16[16,768]{1,0:T(8,128)(2,1)S(1)}, u32[]{:S(2)}, u32[]{:S(2)}) collective-permute-start(bf16[16,768]{1,0:T(8,128)(2,1)S(1)} %copy.23), channel_id=1, source_target_pairs={{12,0},{0,4},{4,8},{8,12},{13,1},{1,5},{5,9},{9,13},{14,2},{2,6},{... | collective-permute-start | bytes 73736 | tf_op jit(solution)/shard_map/while/body/eval_jaxpr/ppermute | solution.py:19
  78.5 7.0 %collective-permute-start = (bf16[16,4096]{1,0:T(8,128)(2,1)S(1)}, bf16[16,4096]{1,0:T(8,128)(2,1)S(1)}, u32[]{:S(2)}, u32[]{:S(2)}) collective-permute-start(bf16[16,4096]{1,0:T(8,128)(2,1)S(1)} %copy.22), channel_id=1, source_target_pairs={{12,0},{0,4},{4,8},{8,12},{13,1},{1,5},{5,9},{9,13},{14,2},{2,6},{... | collective-permute-start | bytes 393224 | tf_op jit(solution)/shard_map/while/body/eval_jaxpr/ppermute | solution.py:19
  85.5 5.6 %collective-permute-start.1 = (bf16[16,768]{1,0:T(8,128)(2,1)S(1)}, bf16[16,768]{1,0:T(8,128)(2,1)S(1)}, u32[]{:S(2)}, u32[]{:S(2)}) collective-permute-start(bf16[16,768]{1,0:T(8,128)(2,1)S(1)} %copy.23), channel_id=1, source_target_pairs={{12,0},{0,4},{4,8},{8,12},{13,1},{1,5},{5,9},{9,13},{14,2},{2,6},{... | collective-permute-start | bytes 73736 | tf_op jit(solution)/shard_map/while/body/eval_jaxpr/ppermute | solution.py:19
  85.5 7.0 %collective-permute-start = (bf16[16,4096]{1,0:T(8,128)(2,1)S(1)}, bf16[16,4096]{1,0:T(8,128)(2,1)S(1)}, u32[]{:S(2)}, u32[]{:S(2)}) collective-permute-start(bf16[16,4096]{1,0:T(8,128)(2,1)S(1)} %copy.22), channel_id=1, source_target_pairs={{12,0},{0,4},{4,8},{8,12},{13,1},{1,5},{5,9},{9,13},{14,2},{2,6},{... | collective-permute-start | bytes 393224 | tf_op jit(solution)/shard_map/while/body/eval_jaxpr/ppermute | solution.py:19
  157.7 5.9 %collective-permute-start.2 = (f32[16,768]{1,0:T(8,128)S(1)}, f32[16,768]{1,0:T(8,128)S(1)}, u32[]{:S(2)}, u32[]{:S(2)}) collective-permute-start(f32[16,768]{1,0:T(8,128)S(1)} %fusion.56), channel_id=1, source_target_pairs={{12,0},{0,4},{4,8},{8,12},{13,1},{1,5},{5,9},{9,13},{14,2},{2,6},{... | collective-permute-start | bytes 147464 | tf_op jit(solution)/shard_map/while/body/eval_jaxpr/ppermute | solution.py:19
  163.8 5.9 %collective-permute-start.2 = (f32[16,768]{1,0:T(8,128)S(1)}, f32[16,768]{1,0:T(8,128)S(1)}, u32[]{:S(2)}, u32[]{:S(2)}) collective-permute-start(f32[16,768]{1,0:T(8,128)S(1)} %fusion.56), channel_id=1, source_target_pairs={{12,0},{0,4},{4,8},{8,12},{13,1},{1,5},{5,9},{9,13},{14,2},{2,6},{... | collective-permute-start | bytes 147464 | tf_op jit(solution)/shard_map/while/body/eval_jaxpr/ppermute | solution.py:19
  169.9 5.9 %collective-permute-start.2 = (f32[16,768]{1,0:T(8,128)S(1)}, f32[16,768]{1,0:T(8,128)S(1)}, u32[]{:S(2)}, u32[]{:S(2)}) collective-permute-start(f32[16,768]{1,0:T(8,128)S(1)} %fusion.56), channel_id=1, source_target_pairs={{12,0},{0,4},{4,8},{8,12},{13,1},{1,5},{5,9},{9,13},{14,2},{2,6},{... | collective-permute-start | bytes 147464 | tf_op jit(solution)/shard_map/while/body/eval_jaxpr/ppermute | solution.py:19
  176.0 5.9 %collective-permute-start.2 = (f32[16,768]{1,0:T(8,128)S(1)}, f32[16,768]{1,0:T(8,128)S(1)}, u32[]{:S(2)}, u32[]{:S(2)}) collective-permute-start(f32[16,768]{1,0:T(8,128)S(1)} %fusion.56), channel_id=1, source_target_pairs={{12,0},{0,4},{4,8},{8,12},{13,1},{1,5},{5,9},{9,13},{14,2},{2,6},{... | collective-permute-start | bytes 147464 | tf_op jit(solution)/shard_map/while/body/eval_jaxpr/ppermute | solution.py:19
where the time goes:
time: 194 us; the launch traced here: 193 us
  blocking collectives  117 us (60%)
  waiting for transfers between devices  28.9 us (15%)
  matrix products  16.6 us (9%)
  local copies, waits for them, and re-layouts  15.4 us (8%)
  starting transfers between devices  12.3 us (6%)
    unnamed x1, blocking collectives  57.6 us
    all_gather x1, blocking collectives, body(): whole_panel = lax.all_gather(t_query, 'width', axis=1, tiled=True)  48 us
    ppermute x10, waiting for transfers between devices, shifted(): return lax.ppermute(block, axis, route)  28.9 us
    dot_general x4, matrix products, teacher_scores(): jnp.einsum('qd,pd->qp', panel, t_rows, preferred_element_type=jnp.float32)  12.9 us
    psum x1, blocking collectives, body(): grad_query = lax.psum(width_part, 'width')  11.1 us
    ppermute x10, starting transfers between devices, shifted(): return lax.ppermute(block, axis, route)  7.36 us
    while x1, local copies, waits for them, and re-layouts, body(): panels, stores = lax.fori_loop(0, blocks - 1, turn, (panels, stores))  6.46 us
    all_to_all x1, local copies, waits for them, and re-layouts, body(): lax.all_to_all(t_pass, 'width', split_axis=0, concat_axis=1, tiled=True)  6.2 us
  transfers between devices with their start and end apart: 11, of which 9 were waited for; matrix products, arithmetic and copies ran while one was open for 7% of the time, Pallas kernels for 0%

commit v1 on v0

v1 whole, which is shorter than its diff:
```python
import functools
import math

import jax
import jax.numpy as jnp
from jax import lax
from jax.experimental import pallas as pl
from jax.experimental.pallas import tpu as pltpu
from jax.sharding import PartitionSpec as P

TEMPER = 2.0
MASK_FILL = -1e30
LANES = 128
MESH_ID = pl.DeviceIdType.MESH
NT = (((1,), (1,)), ((), ()))
TN = (((0,), (0,)), ((), ()))


def kernel(
    sizes,
    tq_ref,
    tp_ref,
    sq_ref,
    sp_ref,
    pos_ref,
    doc_ref,
    gq_ref,
    gp_ref,
    tq_all,
    tp_v,
    sq_all,
    sp_v,
    pos_v,
    doc_v,
    mate_out,
    mate_in,
    far_out,
    far_in,
    stat_w,
    stat_b,
    piece_out,
    piece_in,
    block_out,
    block_in,
    final_in,
    gp_v,
    local_sem,
    tq_send,
    tq_recv,
    sq_send,
    sq_recv,
    mate_send,
    mate_recv,
    far_send,
    far_recv,
    statw_send,
    statw_recv,
    statb_send,
    statb_recv,
    piece_send,
    piece_recv,
    block_send,
    block_recv,
    final_send,
    final_recv,
):
    blocks, widths, t_width, s_width = sizes
    panel = sq_ref.shape[0]
    queries = blocks * panel
    own = sp_ref.shape[0]
    outer = widths // 2
    t_scale = TEMPER / math.sqrt(t_width)
    s_scale = TEMPER / math.sqrt(s_width)
    b = lax.axis_index("blk")
    w = lax.axis_index("width")
    side = lax.rem(w, 2)
    chip = w // 2
    pending = []

    barrier = pltpu.get_barrier_semaphore()
    for k in range(1, blocks):
        pl.semaphore_signal(
            barrier, inc=1, device_id={"blk": lax.rem(b + k, blocks)}, device_id_type=MESH_ID
        )
    for k in range(1, widths):
        pl.semaphore_signal(
            barrier, inc=1, device_id={"width": lax.rem(w + k, widths)}, device_id_type=MESH_ID
        )

    tq_own = pltpu.make_async_copy(tq_ref, tq_all.at[b], local_sem.at[0])
    sq_own = pltpu.make_async_copy(sq_ref, sq_all.at[b], local_sem.at[1])
    sp_copy = pltpu.make_async_copy(sp_ref, sp_v, local_sem.at[2])
    pos_copy = pltpu.make_async_copy(pos_ref, pos_v, local_sem.at[3])
    doc_copy = pltpu.make_async_copy(doc_ref, doc_v, local_sem.at[4])
    tq_own.start()
    sq_own.start()
    pos_copy.start()
    doc_copy.start()
    tp_copies = []
    for step in range(outer):
        target = lax.rem(chip + 1 + step, outer)
        for part in range(2):
            place = 2 * target + (1 - side if part == 0 else side)
            slot = 2 * step + part
            copy = pltpu.make_async_copy(
                tp_ref.at[pl.ds(pl.multiple_of(place * own, own), own), :],
                tp_v.at[slot],
                local_sem.at[5 + slot],
            )
            copy.start()
            tp_copies.append(copy)
    sp_copy.start()

    pl.semaphore_wait(barrier, blocks + widths - 2)

    def send(src, dst, send_sem, recv_sem, where):
        copy = pltpu.make_async_remote_copy(
            src_ref=src,
            dst_ref=dst,
            send_sem=send_sem,
            recv_sem=recv_sem,
            device_id=where,
            device_id_type=MESH_ID,
        )
        copy.start()
        pending.append(copy)
        return copy

    tq_copies, sq_copies = [], []
    for k in range(1, blocks):
        to = {"blk": lax.rem(b + k, blocks)}
        tq_copies.append(send(tq_ref, tq_all.at[b], tq_send.at[k], tq_recv.at[k], to))
    for k in range(1, blocks):
        to = {"blk": lax.rem(b + k, blocks)}
        sq_copies.append(send(sq_ref, sq_all.at[b], sq_send.at[k], sq_recv.at[k], to))

    eye = lax.broadcasted_iota(jnp.int32, (queries, queries), 0) == lax.broadcasted_iota(
        jnp.int32, (queries, queries), 1
    )

    def to_row(column):
        return jnp.sum(jnp.where(eye, column, 0.0), axis=0, keepdims=True)

    def to_column(row):
        return jnp.sum(jnp.where(eye, row, 0.0), axis=1, keepdims=True)

    pos_copy.wait()
    doc_copy.wait()
    positive = to_column(pos_v[...].astype(jnp.float32)).astype(jnp.int32)
    lane = lax.broadcasted_iota(jnp.int32, (1, LANES), 1)

    def look(row, found):
        docs = doc_v[pl.ds(row, 1), :]
        return jnp.where(positive - row * LANES == lane, docs, found)

    found = lax.fori_loop(
        0, doc_v.shape[0], look, jnp.full((queries, LANES), -1, jnp.int32), unroll=4
    )
    target_docs = jnp.max(found.astype(jnp.float32), axis=1, keepdims=True).astype(jnp.int32)
    first_row = (b * widths + w) * own
    first_line = (b * widths + w) * (own // LANES)
    docs = jnp.concatenate(
        [doc_v[pl.ds(first_line + j, 1), :] for j in range(own // LANES)], axis=1
    )
    columns = first_row + lax.broadcasted_iota(jnp.int32, (1, own), 1)
    is_positive = columns == positive
    masked = (docs == target_docs) & jnp.logical_not(is_positive)

    tq_own.wait()
    for copy in tq_copies:
        copy.wait_recv()
    panels = tq_all[...].reshape(queries, tq_all.shape[2])

    def partial_scores(slot):
        tp_copies[slot].wait()
        return lax.dot_general(panels, tp_v[slot], NT, preferred_element_type=jnp.float32)

    teach = None
    far_copies = []
    for step in range(outer):
        mate_out[step] = partial_scores(2 * step)
        mate_copy = send(
            mate_out.at[step],
            mate_in.at[step],
            mate_send.at[step],
            mate_recv.at[step],
            {"width": w + 1 - 2 * side},
        )
        kept = partial_scores(2 * step + 1)
        mate_copy.wait_recv()
        kept = kept + mate_in[step]
        if step < outer - 1:
            far_out[step] = kept
            far_copies.append(
                send(
                    far_out.at[step],
                    far_in.at[step],
                    far_send.at[step],
                    far_recv.at[step],
                    {"width": 2 * lax.rem(chip + 1 + step, outer) + side},
                )
            )
        else:
            teach = kept

    def totals(filled):
        highest = jnp.max(filled, axis=1, keepdims=True)
        summed = jnp.sum(jnp.exp(filled - highest), axis=1, keepdims=True)
        return to_row(highest), to_row(summed)

    sq_own.wait()
    for copy in sq_copies:
        copy.wait_recv()
    sp_copy.wait()
    queries_all = sq_all[...].reshape(queries, s_width)
    learn = lax.dot_general(queries_all, sp_v[...], NT, preferred_element_type=jnp.float32)
    learn_fill = jnp.where(masked, MASK_FILL, learn * s_scale)
    learn_high, learn_sum = totals(learn_fill)

    for step, copy in enumerate(far_copies):
        copy.wait_recv()
        teach = teach + far_in[step]
    teach_fill = jnp.where(masked, MASK_FILL, teach * t_scale)
    teach_high, teach_sum = totals(teach_fill)

    def write(ref, values):
        for i, value in enumerate(values):
            ref[i : i + 1, :queries] = value

    def combine(ref, count):
        merged = []
        for place in (0, 2):
            highs = [ref[i][place : place + 1, :queries] for i in range(count)]
            sums = [ref[i][place + 1 : place + 2, :queries] for i in range(count)]
            high = functools.reduce(jnp.maximum, highs)
            total = functools.reduce(
                jnp.add, [s * jnp.exp(h - high) for h, s in zip(highs, sums)]
            )
            merged += [high, total]
        return merged

    def exchange(ref, axis, count, me, send_sems, recv_sems):
        copies = []
        for k in range(1, count):
            copies.append(
                send(
                    ref.at[0],
                    ref.at[k],
                    send_sems.at[k],
                    recv_sems.at[k],
                    {axis: lax.rem(me + k, count)},
                )
            )
        for copy in copies:
            copy.wait_recv()

    stat_w[0] = jnp.zeros(stat_w.shape[1:], jnp.float32)
    stat_b[0] = jnp.zeros(stat_b.shape[1:], jnp.float32)
    write(stat_w.at[0], (teach_high, teach_sum, learn_high, learn_sum))
    exchange(stat_w, "width", widths, w, statw_send, statw_recv)
    write(stat_b.at[0], combine(stat_w, widths))
    exchange(stat_b, "blk", blocks, b, statb_send, statb_recv)
    teach_high, teach_sum, learn_high, learn_sum = combine(stat_b, blocks)
    teach_log = to_column(teach_high + jnp.log(teach_sum))
    learn_log = to_column(learn_high + jnp.log(learn_sum))
    teach_probs = jnp.exp(teach_fill - teach_log)
    learn_probs = jnp.exp(learn_fill - learn_log)
    slope = (2.0 * learn_probs - teach_probs - is_positive.astype(jnp.float32)).astype(
        jnp.bfloat16
    )

    grad = jnp.dot(slope, sp_v[...], preferred_element_type=jnp.float32) * s_scale
    rows = panel // 2
    cols = s_width // outer
    for place in range(widths):
        half, col = place % 2, place // 2
        for block in range(blocks):
            top = block * panel + half * rows
            piece_out[place, block] = grad[top : top + rows, col * cols : (col + 1) * cols]
    piece_copies = []
    for k in range(1, widths):
        to = lax.rem(w + k, widths)
        piece_copies.append(
            send(
                piece_out.at[to],
                piece_in.at[k],
                piece_send.at[k],
                piece_recv.at[k],
                {"width": to},
            )
        )

    tall = min(own, 128)
    gp_copies = []

    def passage_part(i):
        part = lax.dot_general(
            slope[:, i * tall : (i + 1) * tall],
            queries_all,
            TN,
            preferred_element_type=jnp.float32,
        )
        gp_v[i * tall : (i + 1) * tall, :] = part * s_scale
        copy = pltpu.make_async_copy(
            gp_v.at[i * tall : (i + 1) * tall, :],
            gp_ref.at[i * tall : (i + 1) * tall, :],
            local_sem.at[5 + widths + i],
        )
        copy.start()
        gp_copies.append(copy)

    parts = own // tall
    for i in range(parts // 2):
        passage_part(i)

    total = piece_out[w]
    for k, copy in enumerate(piece_copies):
        copy.wait_recv()
        total = total + piece_in[k + 1]
    block_out[...] = total
    block_copies = []
    for k in range(1, blocks):
        to = lax.rem(b + k, blocks)
        block_copies.append(
            send(
                block_out.at[to],
                block_in.at[k],
                block_send.at[k],
                block_recv.at[k],
                {"blk": to},
            )
        )
    for i in range(parts // 2, parts):
        passage_part(i)
    total = block_out[b]
    for k, copy in enumerate(block_copies):
        copy.wait_recv()
        total = total + block_in[k + 1]
    final_in[w] = total
    final_copies = []
    for k in range(1, widths):
        final_copies.append(
            send(
                final_in.at[w],
                final_in.at[w],
                final_send.at[k],
                final_recv.at[k],
                {"width": lax.rem(w + k, widths)},
            )
        )
    for copy in final_copies:
        copy.wait_recv()
    for place in range(widths):
        half, col = place % 2, place // 2
        gq_ref[half * rows : (half + 1) * rows, col * cols : (col + 1) * cols] = final_in[place]

    for copy in gp_copies:
        copy.wait()
    for copy in pending:
        copy.wait_send()


def solution(mesh):
    blocks, widths = mesh.shape["blk"], mesh.shape["width"]

    def body(t_query, t_pass, s_query, s_pass, positive, doc_ids):
        panel, s_width = s_query.shape
        own = s_pass.shape[0]
        feats = t_query.shape[1]
        queries = blocks * panel
        outer = widths // 2
        rows, cols = panel // 2, s_width // outer
        f32, bf16 = jnp.float32, jnp.bfloat16
        lines = doc_ids.shape[0] // LANES
        dma = pltpu.SemaphoreType.DMA
        any_space = pl.BlockSpec(memory_space=pl.ANY)
        far = max(outer - 1, 1)
        stat_lanes = max(queries, LANES)
        return pl.pallas_call(
            functools.partial(kernel, (blocks, widths, feats * widths, s_width)),
            out_shape=(
                jax.ShapeDtypeStruct((panel, s_width), f32),
                jax.ShapeDtypeStruct((own, s_width), f32),
            ),
            in_specs=[any_space] * 6,
            out_specs=(pl.BlockSpec(memory_space=pltpu.VMEM), any_space),
            scratch_shapes=[
                pltpu.VMEM((blocks, panel, feats), bf16),
                pltpu.VMEM((widths, own, feats), bf16),
                pltpu.VMEM((blocks, panel, s_width), bf16),
                pltpu.VMEM((own, s_width), bf16),
                pltpu.VMEM((1, queries), jnp.int32),
                pltpu.VMEM((lines, LANES), jnp.int32),
                pltpu.VMEM((outer, queries, own), f32),
                pltpu.VMEM((outer, queries, own), f32),
                pltpu.VMEM((far, queries, own), f32),
                pltpu.VMEM((far, queries, own), f32),
                pltpu.VMEM((widths, 8, stat_lanes), f32),
                pltpu.VMEM((blocks, 8, stat_lanes), f32),
                pltpu.VMEM((widths, blocks, rows, cols), f32),
                pltpu.VMEM((widths, blocks, rows, cols), f32),
                pltpu.VMEM((blocks, rows, cols), f32),
                pltpu.VMEM((blocks, rows, cols), f32),
                pltpu.VMEM((widths, rows, cols), f32),
                pltpu.VMEM((own, s_width), f32),
                dma((5 + widths + own // LANES,)),
                dma((blocks,)),
                dma((blocks,)),
                dma((blocks,)),
                dma((blocks,)),
                dma((outer,)),
                dma((outer,)),
                dma((far,)),
                dma((far,)),
                dma((widths,)),
                dma((widths,)),
                dma((blocks,)),
                dma((blocks,)),
                dma((widths,)),
                dma((widths,)),
                dma((blocks,)),
                dma((blocks,)),
                dma((widths,)),
                dma((widths,)),
            ],
            compiler_params=pltpu.CompilerParams(
                collective_id=0, has_side_effects=True, vmem_limit_bytes=40 * 1024 * 1024
            ),
        )(
            t_query,
            t_pass,
            s_query,
            s_pass,
            positive.reshape(1, queries),
            doc_ids.reshape(lines, LANES),
        )

    placed = (
        P(("groups", "blk"), "width"),
        P(("groups", "blk"), "width"),
        P(("groups", "blk"), None),
        P(("groups", "blk", "width"), None),
        P("groups"),
        P("groups"),
    )
    return jax.shard_map(
        body,
        mesh=mesh,
        in_specs=placed,
        out_specs=(P(("groups", "blk"), None), P(("groups", "blk", "width"), None)),
        check_vma=False,
    )
```

time: 194 us -> 41.4 us (0.21)
  blocking collectives: 117 us -> 0 us
  Pallas kernels: 0 us -> 32.4 us
  waiting for transfers between devices: 28.9 us -> 0 us
  matrix products: 16.6 us -> 0 us
  starting transfers between devices: 12.3 us -> 0 us
  local copies, waits for them, and re-layouts: 15.4 us -> 7.98 us
    unnamed x1 -> x0, blocking collectives: 57.6 us -> none
    all_gather x1 -> x0, blocking collectives: 48 us -> none  [body(): whole_panel = lax.all_gather(t_query, 'width', axis=1, tiled=True)]
    pallas_call x0 -> x1, Pallas kernels: none -> 32.4 us  [body(): pl.pallas_call(functools.partial(kernel, (blocks, widths, feats * widths,...]
    ppermute x10 -> x0, waiting for transfers between devices: 28.9 us -> none  [shifted(): return lax.ppermute(block, axis, route)]
    dot_general x13 -> x0, matrix products: 16.6 us -> none  [the longest x4 12.9 us: teacher_scores(): jnp.einsum('qd,pd->qp', panel, t_rows, preferred_element_type=jnp.float32)]
    psum x1 -> x0, blocking collectives: 11.1 us -> none  [body(): grad_query = lax.psum(width_part, 'width')]
    ppermute x10 -> x0, starting transfers between devices: 7.36 us -> none  [shifted(): return lax.ppermute(block, axis, route)]
    while x1 -> x0, local copies, waits for them, and re-layouts: 6.46 us -> none  [body(): panels, stores = lax.fori_loop(0, blocks - 1, turn, (panels, stores))]
  transfers between devices with their start and end apart: 11 -> 0, of which waited for: 9 -> 0; matrix products, arithmetic and copies ran while one was open for 7% -> 0% of each run, Pallas kernels for 0% -> 0%
where the time goes in v1:
time: 41.4 us; the launch traced here: 41 us
  Pallas kernels  32.4 us (78%)
  local copies, waits for them, and re-layouts  7.98 us (19%)
  between operations  0.65 us (2%)
    pallas_call x1, Pallas kernels, body(): pl.pallas_call(functools.partial(kernel, (blocks, widths, feats * widths,...  32.4 us
    unnamed x14, local copies, waits for them, and re-layouts  7.98 us

profile of v1, /device:TPU:0, one launch (start us, length us, event | category | flops | bytes accessed | tf_op | source)
XLA Modules:
  0.0 41.0 jit_solution(4441871219059064595)
XLA Ops:
  0.6 0.0 copy-start
  0.6 2.2 %copy-done = bf16[2048,1024]{1,0:T(8,128)(2,1)S(1)} copy-done((bf16[2048,1024]{1,0:T(8,128)(2,1)S(1)}, bf16[2048,1024]{1,0:T(8,128)(2,1)}, u32[]{:S(2)}) %copy-start) | copy-done | bytes 4194328
  2.8 0.0 copy-start.1
  2.8 1.1 %copy-done.1 = bf16[512,768]{1,0:T(8,128)(2,1)S(1)} copy-done((bf16[512,768]{1,0:T(8,128)(2,1)S(1)}, bf16[512,768]{1,0:T(8,128)(2,1)}, u32[]{:S(2)}) %copy-start.1) | copy-done | bytes 786456
  4.0 0.0 copy-start.2
  4.0 0.8 %copy-done.2 = bf16[16,1024]{1,0:T(8,128)(2,1)S(1)} copy-done((bf16[16,1024]{1,0:T(8,128)(2,1)S(1)}, bf16[16,1024]{1,0:T(8,128)(2,1)}, u32[]{:S(2)}) %copy-start.2) | copy-done | bytes 32792
  4.7 0.0 copy-start.3
  4.7 0.8 %copy-done.3 = s32[8192]{0:T(1024)S(1)} copy-done((s32[8192]{0:T(1024)S(1)}, s32[8192]{0:T(1024)}, u32[]{:S(2)}) %copy-start.3) | copy-done | bytes 32792
  5.5 0.0 copy-start.4
  5.5 0.7 %copy-done.4 = bf16[16,768]{1,0:T(8,128)(2,1)S(1)} copy-done((bf16[16,768]{1,0:T(8,128)(2,1)S(1)}, bf16[16,768]{1,0:T(8,128)(2,1)}, u32[]{:S(2)}) %copy-start.4) | copy-done | bytes 24600
  6.2 0.0 copy-start.5
  6.2 0.7 %copy-done.5 = s32[64]{0:T(128)S(1)} copy-done((s32[64]{0:T(128)S(1)}, s32[64]{0:T(128)}, u32[]{:S(2)}) %copy-start.5) | copy-done | bytes 280
  6.9 32.4 %shard_map.77 = (f32[16,768]{1,0:T(8,128)S(1)}, f32[512,768]{1,0:T(8,128)S(1)}) custom-call(bf16[16,1024]{1,0:T(8,128)(2,1)S(1)} %copy-done.2, bf16[2048,1024]{1,0:T(8,128)(2,1)S(1)} %copy-done, bf16[16,768]{1,0:T(8,128)(2,1)S(1)} %copy-done.4, bf16[512,768]{1,0:T(8,128)(2,1)S(1)} %copy-done.1, s32[1,64]{1,0:T(1,128)S(1)} %bitcast.3, s32[64,128]{1,0:T(8,128)S(1)} %bitcast.2), custom_call_target="tpu_custom_call" | custom-call | tf_op jit(solution)/shard_map/pallas_call | solution.py:379
  39.3 0.6 %copy.10 = f32[16,768]{1,0:T(8,128)} copy(f32[16,768]{1,0:T(8,128)S(1)} %get-tuple-element.4) | data formatting | bytes 98304
  39.9 1.1 %copy.11 = f32[512,768]{1,0:T(8,128)} copy(f32[512,768]{1,0:T(8,128)S(1)} %get-tuple-element.5) | data formatting | bytes 3145728
Async XLA Ops:
  0.6 2.2 %copy-start = (bf16[2048,1024]{1,0:T(8,128)(2,1)S(1)}, bf16[2048,1024]{1,0:T(8,128)(2,1)}, u32[]{:S(2)}) copy-start(bf16[2048,1024]{1,0:T(8,128)(2,1)} %tp_ref.1) | copy-start | bytes 12582916
  2.8 1.1 %copy-start.1 = (bf16[512,768]{1,0:T(8,128)(2,1)S(1)}, bf16[512,768]{1,0:T(8,128)(2,1)}, u32[]{:S(2)}) copy-start(bf16[512,768]{1,0:T(8,128)(2,1)} %sp_ref.1) | copy-start | bytes 2359300
  4.0 0.8 %copy-start.2 = (bf16[16,1024]{1,0:T(8,128)(2,1)S(1)}, bf16[16,1024]{1,0:T(8,128)(2,1)}, u32[]{:S(2)}) copy-start(bf16[16,1024]{1,0:T(8,128)(2,1)} %tq_ref.1) | copy-start | bytes 98308
  4.7 0.8 %copy-start.3 = (s32[8192]{0:T(1024)S(1)}, s32[8192]{0:T(1024)}, u32[]{:S(2)}) copy-start(s32[8192]{0:T(1024)} %param.11) | copy-start | bytes 98308
  5.5 0.7 %copy-start.4 = (bf16[16,768]{1,0:T(8,128)(2,1)S(1)}, bf16[16,768]{1,0:T(8,128)(2,1)}, u32[]{:S(2)}) copy-start(bf16[16,768]{1,0:T(8,128)(2,1)} %sq_ref.1) | copy-start | bytes 73732
  6.2 0.7 %copy-start.5 = (s32[64]{0:T(128)S(1)}, s32[64]{0:T(128)}, u32[]{:S(2)}) copy-start(s32[64]{0:T(128)} %param.10) | copy-start | bytes 772

commit v2 on v1

--- a/solution.py
+++ b/solution.py
@@ -25,7 +25,8 @@
     pos_ref,
     doc_ref,
     gq_ref,
-    gp_ref,
+    slope_ref,
+    queries_ref,
     tq_all,
     tp_v,
     sq_all,
@@ -36,14 +37,11 @@
     mate_in,
     far_out,
     far_in,
-    stat_w,
-    stat_b,
+    stat,
     piece_out,
     piece_in,
-    block_out,
-    block_in,
     final_in,
-    gp_v,
+    slope_v,
     local_sem,
     tq_send,
     tq_recv,
@@ -53,14 +51,10 @@
     mate_recv,
     far_send,
     far_recv,
-    statw_send,
-    statw_recv,
-    statb_send,
-    statb_recv,
+    stat_send,
+    stat_recv,
     piece_send,
     piece_recv,
-    block_send,
-    block_recv,
     final_send,
     final_recv,
 ):
@@ -77,15 +71,33 @@
     chip = w // 2
     pending = []
 
+    group = blocks * widths
+    me = b * widths + w
+
+    def peer(k):
+        other = lax.rem(me + k, group)
+        return other, {"blk": other // widths, "width": lax.rem(other, widths)}
+
+    def over(first, last, step, carry):
+        if last - first < 16:
+            for k in range(first, last):
+                carry = step(k, carry)
+            return carry
+        return lax.fori_loop(first, last, step, carry)
+
+    def each(step):
+        def run(k, carry):
+            step(k)
+            return carry
+
+        over(1, group, run, 0)
+
     barrier = pltpu.get_barrier_semaphore()
-    for k in range(1, blocks):
-        pl.semaphore_signal(
-            barrier, inc=1, device_id={"blk": lax.rem(b + k, blocks)}, device_id_type=MESH_ID
-        )
-    for k in range(1, widths):
-        pl.semaphore_signal(
-            barrier, inc=1, device_id={"width": lax.rem(w + k, widths)}, device_id_type=MESH_ID
-        )
+    each(
+        lambda k: pl.semaphore_signal(
+            barrier, inc=1, device_id=peer(k)[1], device_id_type=MESH_ID
+        )
+    )
 
     tq_own = pltpu.make_async_copy(tq_ref, tq_all.at[b], local_sem.at[0])
     sq_own = pltpu.make_async_copy(sq_ref, sq_all.at[b], local_sem.at[1])
@@ -111,7 +123,7 @@
             tp_copies.append(copy)
     sp_copy.start()
 
-    pl.semaphore_wait(barrier, blocks + widths - 2)
+    pl.semaphore_wait(barrier, group - 1)
 
     def send(src, dst, send_sem, recv_sem, where):
         copy = pltpu.make_async_remote_copy(
@@ -130,9 +142,6 @@
     for k in range(1, blocks):
         to = {"blk": lax.rem(b + k, blocks)}
         tq_copies.append(send(tq_ref, tq_all.at[b], tq_send.at[k], tq_recv.at[k], to))
-    for k in range(1, blocks):
-        to = {"blk": lax.rem(b + k, blocks)}
-        sq_copies.append(send(sq_ref, sq_all.at[b], sq_send.at[k], sq_recv.at[k], to))
 
     eye = lax.broadcasted_iota(jnp.int32, (queries, queries), 0) == lax.broadcasted_iota(
         jnp.int32, (queries, queries), 1
@@ -169,6 +178,9 @@
     tq_own.wait()
     for copy in tq_copies:
         copy.wait_recv()
+    for k in range(1, blocks):
+        to = {"blk": lax.rem(b + k, blocks)}
+        sq_copies.append(send(sq_ref, sq_all.at[b], sq_send.at[k], sq_recv.at[k], to))
     panels = tq_all[...].reshape(queries, tq_all.shape[2])
 
     def partial_scores(slot):
@@ -223,46 +235,33 @@
     teach_fill = jnp.where(masked, MASK_FILL, teach * t_scale)
     teach_high, teach_sum = totals(teach_fill)
 
-    def write(ref, values):
-        for i, value in enumerate(values):
-            ref[i : i + 1, :queries] = value
-
-    def combine(ref, count):
-        merged = []
-        for place in (0, 2):
-            highs = [ref[i][place : place + 1, :queries] for i in range(count)]
-            sums = [ref[i][place + 1 : place + 2, :queries] for i in range(count)]
-            high = functools.reduce(jnp.maximum, highs)
-            total = functools.reduce(
-                jnp.add, [s * jnp.exp(h - high) for h, s in zip(highs, sums)]
-            )
-            merged += [high, total]
-        return merged
-
-    def exchange(ref, axis, count, me, send_sems, recv_sems):
-        copies = []
-        for k in range(1, count):
-            copies.append(
-                send(
-                    ref.at[0],
-                    ref.at[k],
-                    send_sems.at[k],
-                    recv_sems.at[k],
-                    {axis: lax.rem(me + k, count)},
-                )
-            )
-        for copy in copies:
-            copy.wait_recv()
-
-    stat_w[0] = jnp.zeros(stat_w.shape[1:], jnp.float32)
-    stat_b[0] = jnp.zeros(stat_b.shape[1:], jnp.float32)
-    write(stat_w.at[0], (teach_high, teach_sum, learn_high, learn_sum))
-    exchange(stat_w, "width", widths, w, statw_send, statw_recv)
-    write(stat_b.at[0], combine(stat_w, widths))
-    exchange(stat_b, "blk", blocks, b, statb_send, statb_recv)
-    teach_high, teach_sum, learn_high, learn_sum = combine(stat_b, blocks)
-    teach_log = to_column(teach_high + jnp.log(teach_sum))
-    learn_log = to_column(learn_high + jnp.log(learn_sum))
+    for i, value in enumerate((teach_high, learn_high, teach_sum, learn_sum)):
+        stat[0, i : i + 1, :queries] = value
+
+    def stat_copy(k):
+        return pltpu.make_async_remote_copy(
+            src_ref=stat.at[0],
+            dst_ref=stat.at[k],
+            send_sem=stat_send.at[k],
+            recv_sem=stat_recv.at[k],
+            device_id=peer(k)[1],
+            device_id_type=MESH_ID,
+        )
+
+    each(lambda k: stat_copy(k).start())
+    each(lambda k: stat_copy(k).wait_recv())
+
+    def highs(k):
+        return stat[k, 0:2, :queries]
+
+    high = over(1, group, lambda k, best: jnp.maximum(best, highs(k)), highs(0))
+
+    def add_total(k, total):
+        return total + stat[k, 2:4, :queries] * jnp.exp(highs(k) - high)
+
+    logs = high + jnp.log(over(0, group, add_total, jnp.zeros((2, queries), jnp.float32)))
+    teach_log = to_column(logs[0:1])
+    learn_log = to_column(logs[1:2])
     teach_probs = jnp.exp(teach_fill - teach_log)
     learn_probs = jnp.exp(learn_fill - learn_log)
     slope = (2.0 * learn_probs - teach_probs - is_positive.astype(jnp.float32)).astype(
@@ -272,70 +271,35 @@
     grad = jnp.dot(slope, sp_v[...], preferred_element_type=jnp.float32) * s_scale
     rows = panel // 2
     cols = s_width // outer
-    for place in range(widths):
-        half, col = place % 2, place // 2
-        for block in range(blocks):
+    for block in range(blocks):
+        for place in range(widths):
+            half, col = place % 2, place // 2
             top = block * panel + half * rows
-            piece_out[place, block] = grad[top : top + rows, col * cols : (col + 1) * cols]
-    piece_copies = []
-    for k in range(1, widths):
-        to = lax.rem(w + k, widths)
-        piece_copies.append(
-            send(
-                piece_out.at[to],
-                piece_in.at[k],
-                piece_send.at[k],
-                piece_recv.at[k],
-                {"width": to},
-            )
-        )
-
-    tall = min(own, 128)
-    gp_copies = []
-
-    def passage_part(i):
-        part = lax.dot_general(
-            slope[:, i * tall : (i + 1) * tall],
-            queries_all,
-            TN,
-            preferred_element_type=jnp.float32,
-        )
-        gp_v[i * tall : (i + 1) * tall, :] = part * s_scale
-        copy = pltpu.make_async_copy(
-            gp_v.at[i * tall : (i + 1) * tall, :],
-            gp_ref.at[i * tall : (i + 1) * tall, :],
-            local_sem.at[5 + widths + i],
-        )
-        copy.start()
-        gp_copies.append(copy)
-
-    parts = own // tall
-    for i in range(parts // 2):
-        passage_part(i)
-
-    total = piece_out[w]
-    for k, copy in enumerate(piece_copies):
-        copy.wait_recv()
-        total = total + piece_in[k + 1]
-    block_out[...] = total
-    block_copies = []
-    for k in range(1, blocks):
-        to = lax.rem(b + k, blocks)
-        block_copies.append(
-            send(
-                block_out.at[to],
-                block_in.at[k],
-                block_send.at[k],
-                block_recv.at[k],
-                {"blk": to},
-            )
-        )
-    for i in range(parts // 2, parts):
-        passage_part(i)
-    total = block_out[b]
-    for k, copy in enumerate(block_copies):
-        copy.wait_recv()
-        total = total + block_in[k + 1]
+            piece_out[block * widths + place] = grad[
+                top : top + rows, col * cols : (col + 1) * cols
+            ]
+
+    def piece_copy(k):
+        other, to = peer(k)
+        return pltpu.make_async_remote_copy(
+            src_ref=piece_out.at[other],
+            dst_ref=piece_in.at[k],
+            send_sem=piece_send.at[k],
+            recv_sem=piece_recv.at[k],
+            device_id=to,
+            device_id_type=MESH_ID,
+        )
+
+    each(lambda k: piece_copy(k).start())
+
+    slope_v[...] = slope
+    slope_copy = pltpu.make_async_copy(slope_v, slope_ref, local_sem.at[5 + widths])
+    queries_copy = pltpu.make_async_copy(sq_all, queries_ref, local_sem.at[6 + widths])
+    slope_copy.start()
+    queries_copy.start()
+
+    each(lambda k: piece_copy(k).wait_recv())
+    total = over(1, group, lambda k, total: total + piece_in[k], piece_out[me])
     final_in[w] = total
     final_copies = []
     for k in range(1, widths):
@@ -354,10 +318,12 @@
         half, col = place % 2, place // 2
         gq_ref[half * rows : (half + 1) * rows, col * cols : (col + 1) * cols] = final_in[place]
 
-    for copy in gp_copies:
-        copy.wait()
+    slope_copy.wait()
+    queries_copy.wait()
     for copy in pending:
         copy.wait_send()
+    each(lambda k: stat_copy(k).wait_send())
+    each(lambda k: piece_copy(k).wait_send())
 
 
 def solution(mesh):
@@ -370,20 +336,23 @@
         queries = blocks * panel
         outer = widths // 2
         rows, cols = panel // 2, s_width // outer
+        group = blocks * widths
         f32, bf16 = jnp.float32, jnp.bfloat16
         lines = doc_ids.shape[0] // LANES
         dma = pltpu.SemaphoreType.DMA
-        any_space = pl.BlockSpec(memory_space=pl.ANY)
+        any_space = pl.BlockSpec(memory_space=pltpu.HBM)
         far = max(outer - 1, 1)
         stat_lanes = max(queries, LANES)
-        return pl.pallas_call(
+        vmem_space = pl.BlockSpec(memory_space=pltpu.VMEM)
+        grad_query, slope, queries_all = pl.pallas_call(
             functools.partial(kernel, (blocks, widths, feats * widths, s_width)),
             out_shape=(
                 jax.ShapeDtypeStruct((panel, s_width), f32),
-                jax.ShapeDtypeStruct((own, s_width), f32),
+                jax.ShapeDtypeStruct((queries, own), bf16),
+                jax.ShapeDtypeStruct((blocks, panel, s_width), bf16),
             ),
             in_specs=[any_space] * 6,
-            out_specs=(pl.BlockSpec(memory_space=pltpu.VMEM), any_space),
+            out_specs=(vmem_space, any_space, any_space),
             scratch_shapes=[
                 pltpu.VMEM((blocks, panel, feats), bf16),
                 pltpu.VMEM((widths, own, feats), bf16),
@@ -395,15 +364,12 @@
                 pltpu.VMEM((outer, queries, own), f32),
                 pltpu.VMEM((far, queries, own), f32),
                 pltpu.VMEM((far, queries, own), f32),
-                pltpu.VMEM((widths, 8, stat_lanes), f32),
-                pltpu.VMEM((blocks, 8, stat_lanes), f32),
-                pltpu.VMEM((widths, blocks, rows, cols), f32),
-                pltpu.VMEM((widths, blocks, rows, cols), f32),
-                pltpu.VMEM((blocks, rows, cols), f32),
-                pltpu.VMEM((blocks, rows, cols), f32),
+                pltpu.VMEM((group, 4, stat_lanes), f32),
+                pltpu.VMEM((group, rows, cols), f32),
+                pltpu.VMEM((group, rows, cols), f32),
                 pltpu.VMEM((widths, rows, cols), f32),
-                pltpu.VMEM((own, s_width), f32),
-                dma((5 + widths + own // LANES,)),
+                pltpu.VMEM((queries, own), bf16),
+                dma((7 + widths,)),
                 dma((blocks,)),
                 dma((blocks,)),
                 dma((blocks,)),
@@ -412,19 +378,15 @@
                 dma((outer,)),
                 dma((far,)),
                 dma((far,)),
-                dma((widths,)),
-                dma((widths,)),
-                dma((blocks,)),
-                dma((blocks,)),
-                dma((widths,)),
-                dma((widths,)),
-                dma((blocks,)),
-                dma((blocks,)),
+                dma((group,)),
+                dma((group,)),
+                dma((group,)),
+                dma((group,)),
                 dma((widths,)),
                 dma((widths,)),
             ],
             compiler_params=pltpu.CompilerParams(
-                collective_id=0, has_side_effects=True, vmem_limit_bytes=40 * 1024 * 1024
+                collective_id=0, has_side_effects=True, vmem_limit_bytes=60 * 1024 * 1024
             ),
         )(
             t_query,
@@ -434,6 +396,11 @@
             positive.reshape(1, queries),
             doc_ids.reshape(lines, LANES),
         )
+        s_scale = TEMPER / math.sqrt(s_width)
+        grad_passage = s_scale * lax.dot_general(
+            slope, queries_all.reshape(queries, s_width), TN, preferred_element_type=f32
+        )
+        return grad_query, grad_passage
 
     placed = (
         P(("groups", "blk"), "width"),

time: 41.4 us -> 35.8 us (0.86)
  local copies, waits for them, and re-layouts: 7.98 us -> 0.62 us
  matrix products: 0 us -> 2.48 us
  Pallas kernels: 32.4 us -> 31.9 us
    unnamed x14 -> x3, local copies, waits for them, and re-layouts: 7.98 us -> 0.62 us
    dot_general x0 -> x1, matrix products: none -> 2.48 us  [body(): lax.dot_general(slope, queries_all.reshape(queries, s_width), TN, preferr...]
    pallas_call x1, Pallas kernels: 32.4 us -> 31.9 us  [body(): pl.pallas_call(functools.partial(kernel, (blocks, widths, feats * widths,...]
where the time goes in v2:
time: 35.8 us; the launch traced here: 35.6 us
  Pallas kernels  31.9 us (89%)
  matrix products  2.48 us (7%)
  between operations  0.65 us (2%)
  local copies, waits for them, and re-layouts  0.62 us (2%)
    pallas_call x1, Pallas kernels, body(): pl.pallas_call(functools.partial(kernel, (blocks, widths, feats * widths,...  31.9 us
    dot_general x1, matrix products, body(): lax.dot_general(slope, queries_all.reshape(queries, s_width), TN, preferr...  2.48 us

profile of v2, /device:TPU:0, one launch (start us, length us, event | category | flops | bytes accessed | tf_op | source)
XLA Modules:
  0.0 35.6 jit_solution(15480725342784107446)
XLA Ops:
  0.6 31.9 %shard_map.77 = (f32[16,768]{1,0:T(8,128)}, bf16[64,512]{1,0:T(8,128)(2,1)}, bf16[4,16,768]{2,1,0:T(8,128)(2,1)}) custom-call(bf16[16,1024]{1,0:T(8,128)(2,1)} %tq_ref.1, bf16[2048,1024]{1,0:T(8,128)(2,1)} %tp_ref.1, bf16[16,768]{1,0:T(8,128)(2,1)} %sq_ref.1, bf16[512,768]{1,0:T(8,128)(2,1)} %sp_ref.1, s32[1,64]{1,0:T(1,128)} %bitcast.7, s32[64,128]{1,0:T(8,128)} %bitcast.6), custom_call_target="tpu_custom_call" | custom-call | tf_op jit(solution)/shard_map/pallas_call | solution.py:347
  32.5 0.0 copy-start
  32.5 2.5 %convolution_multiply_fusion = f32[512,768]{1,0:T(8,128)} fusion(bf16[64,512]{1,0:T(8,128)(2,1)} %get-tuple-element.6, bf16[64,768]{1,0:T(8,128)(2,1)} %bitcast.5), kind=kOutput, calls=%fused_computation | convolution fusion | flops 50724864 | bytes 1736704 | tf_op jit(solution)/shard_map/dot_general | solution.py:400
  35.0 0.0 copy-done
  35.0 0.6 %copy.9 = f32[16,768]{1,0:T(8,128)} copy(f32[16,768]{1,0:T(8,128)S(1)} %copy-done) | data formatting | bytes 98304
Async XLA Ops:
  32.5 2.5 %copy-start = (f32[16,768]{1,0:T(8,128)S(1)}, f32[16,768]{1,0:T(8,128)}, u32[]{:S(2)}) copy-start(f32[16,768]{1,0:T(8,128)} %get-tuple-element.10) | copy-start | bytes 147460

commit v3 on v2

--- a/solution.py
+++ b/solution.py
@@ -40,7 +40,7 @@
     stat,
     piece_out,
     piece_in,
-    final_in,
+    final,
     slope_v,
     local_sem,
     tq_send,
@@ -183,41 +183,58 @@
         sq_copies.append(send(sq_ref, sq_all.at[b], sq_send.at[k], sq_recv.at[k], to))
     panels = tq_all[...].reshape(queries, tq_all.shape[2])
 
-    def partial_scores(slot):
-        tp_copies[slot].wait()
-        return lax.dot_general(panels, tp_v[slot], NT, preferred_element_type=jnp.float32)
-
-    teach = None
-    far_copies = []
+    wide = own // 2
+    loaded = set()
+
+    def partial_scores(slot, half):
+        if slot not in loaded:
+            loaded.add(slot)
+            tp_copies[slot].wait()
+        part = tp_v[slot, half * wide : (half + 1) * wide, :]
+        return lax.dot_general(panels, part, NT, preferred_element_type=jnp.float32)
+
+    mate_copies, far_copies, kept = [], [], []
+
+    def finish(half, step):
+        place = 2 * step + half
+        mate_copies[place].wait_recv()
+        summed = kept[place] + mate_in[place]
+        if step == outer - 1:
+            return summed
+        far_out[place] = summed
+        far_copies.append(
+            send(
+                far_out.at[place],
+                far_in.at[place],
+                far_send.at[place],
+                far_recv.at[place],
+                {"width": 2 * lax.rem(chip + 1 + step, outer) + side},
+            )
+        )
+
     for step in range(outer):
-        mate_out[step] = partial_scores(2 * step)
-        mate_copy = send(
-            mate_out.at[step],
-            mate_in.at[step],
-            mate_send.at[step],
-            mate_recv.at[step],
-            {"width": w + 1 - 2 * side},
-        )
-        kept = partial_scores(2 * step + 1)
-        mate_copy.wait_recv()
-        kept = kept + mate_in[step]
-        if step < outer - 1:
-            far_out[step] = kept
-            far_copies.append(
+        for half in range(2):
+            place = 2 * step + half
+            mate_out[place] = partial_scores(2 * step, half)
+            mate_copies.append(
                 send(
-                    far_out.at[step],
-                    far_in.at[step],
-                    far_send.at[step],
-                    far_recv.at[step],
-                    {"width": 2 * lax.rem(chip + 1 + step, outer) + side},
+                    mate_out.at[place],
+                    mate_in.at[place],
+                    mate_send.at[place],
+                    mate_recv.at[place],
+                    {"width": w + 1 - 2 * side},
                 )
             )
-        else:
-            teach = kept
+        if step > 0:
+            finish(0, step - 1)
+            finish(1, step - 1)
+        for half in range(2):
+            kept.append(partial_scores(2 * step + 1, half))
 
     def totals(filled):
         highest = jnp.max(filled, axis=1, keepdims=True)
-        summed = jnp.sum(jnp.exp(filled - highest), axis=1, keepdims=True)
+        powers = jnp.exp(filled - highest)
+        summed = jnp.sum(powers, axis=1, keepdims=True)
         return to_row(highest), to_row(summed)
 
     sq_own.wait()
@@ -229,27 +246,33 @@
     learn_fill = jnp.where(masked, MASK_FILL, learn * s_scale)
     learn_high, learn_sum = totals(learn_fill)
 
-    for step, copy in enumerate(far_copies):
+    teach = [finish(half, outer - 1) for half in range(2)]
+    for place, copy in enumerate(far_copies):
         copy.wait_recv()
-        teach = teach + far_in[step]
+        teach[place % 2] = teach[place % 2] + far_in[place]
+    teach = jnp.concatenate(teach, axis=1)
     teach_fill = jnp.where(masked, MASK_FILL, teach * t_scale)
     teach_high, teach_sum = totals(teach_fill)
 
     for i, value in enumerate((teach_high, learn_high, teach_sum, learn_sum)):
         stat[0, i : i + 1, :queries] = value
+
+    def wait_all(ref, sem):
+        whole = ref.at[pl.ds(1, group - 1)]
+        pltpu.make_async_copy(whole, whole, sem).wait()
 
     def stat_copy(k):
         return pltpu.make_async_remote_copy(
             src_ref=stat.at[0],
             dst_ref=stat.at[k],
-            send_sem=stat_send.at[k],
-            recv_sem=stat_recv.at[k],
+            send_sem=stat_send.at[0],
+            recv_sem=stat_recv.at[0],
             device_id=peer(k)[1],
             device_id_type=MESH_ID,
         )
 
     each(lambda k: stat_copy(k).start())
-    each(lambda k: stat_copy(k).wait_recv())
+    wait_all(stat, stat_recv.at[0])
 
     def highs(k):
         return stat[k, 0:2, :queries]
@@ -284,8 +307,8 @@
         return pltpu.make_async_remote_copy(
             src_ref=piece_out.at[other],
             dst_ref=piece_in.at[k],
-            send_sem=piece_send.at[k],
-            recv_sem=piece_recv.at[k],
+            send_sem=piece_send.at[0],
+            recv_sem=piece_recv.at[0],
             device_id=to,
             device_id_type=MESH_ID,
         )
@@ -298,32 +321,41 @@
     slope_copy.start()
     queries_copy.start()
 
-    each(lambda k: piece_copy(k).wait_recv())
+    wait_all(stat, stat_send.at[0])
+    for copy in pending:
+        copy.wait_send()
+    slope_copy.wait()
+    queries_copy.wait()
+    pending.clear()
+    wait_all(piece_in, piece_recv.at[0])
     total = over(1, group, lambda k, total: total + piece_in[k], piece_out[me])
-    final_in[w] = total
+    final[...] = total
+    if len(gq_ref.shape) == 3:
+        place = gq_ref.at[w]
+    else:
+        place = gq_ref.at[
+            pl.ds(pl.multiple_of(side * rows, rows), rows),
+            pl.ds(pl.multiple_of(chip * cols, cols), cols),
+        ]
+    final_own = pltpu.make_async_copy(final, place, local_sem.at[0])
+    final_own.start()
     final_copies = []
     for k in range(1, widths):
         final_copies.append(
             send(
-                final_in.at[w],
-                final_in.at[w],
+                final,
+                place,
                 final_send.at[k],
                 final_recv.at[k],
                 {"width": lax.rem(w + k, widths)},
             )
         )
+    wait_all(piece_in, piece_send.at[0])
+    final_own.wait()
     for copy in final_copies:
         copy.wait_recv()
-    for place in range(widths):
-        half, col = place % 2, place // 2
-        gq_ref[half * rows : (half + 1) * rows, col * cols : (col + 1) * cols] = final_in[place]
-
-    slope_copy.wait()
-    queries_copy.wait()
     for copy in pending:
         copy.wait_send()
-    each(lambda k: stat_copy(k).wait_send())
-    each(lambda k: piece_copy(k).wait_send())
 
 
 def solution(mesh):
@@ -336,6 +368,8 @@
         queries = blocks * panel
         outer = widths // 2
         rows, cols = panel // 2, s_width // outer
+        whole_tiles = rows % 8 == 0 and cols % LANES == 0
+        gq_shape = (panel, s_width) if whole_tiles else (widths, rows, cols)
         group = blocks * widths
         f32, bf16 = jnp.float32, jnp.bfloat16
         lines = doc_ids.shape[0] // LANES
@@ -343,16 +377,15 @@
         any_space = pl.BlockSpec(memory_space=pltpu.HBM)
         far = max(outer - 1, 1)
         stat_lanes = max(queries, LANES)
-        vmem_space = pl.BlockSpec(memory_space=pltpu.VMEM)
         grad_query, slope, queries_all = pl.pallas_call(
             functools.partial(kernel, (blocks, widths, feats * widths, s_width)),
             out_shape=(
-                jax.ShapeDtypeStruct((panel, s_width), f32),
+                jax.ShapeDtypeStruct(gq_shape, f32),
                 jax.ShapeDtypeStruct((queries, own), bf16),
                 jax.ShapeDtypeStruct((blocks, panel, s_width), bf16),
             ),
             in_specs=[any_space] * 6,
-            out_specs=(vmem_space, any_space, any_space),
+            out_specs=(any_space,) * 3,
             scratch_shapes=[
                 pltpu.VMEM((blocks, panel, feats), bf16),
                 pltpu.VMEM((widths, own, feats), bf16),
@@ -360,28 +393,28 @@
                 pltpu.VMEM((own, s_width), bf16),
                 pltpu.VMEM((1, queries), jnp.int32),
                 pltpu.VMEM((lines, LANES), jnp.int32),
-                pltpu.VMEM((outer, queries, own), f32),
-                pltpu.VMEM((outer, queries, own), f32),
-                pltpu.VMEM((far, queries, own), f32),
-                pltpu.VMEM((far, queries, own), f32),
+                pltpu.VMEM((2 * outer, queries, own // 2), f32),
+                pltpu.VMEM((2 * outer, queries, own // 2), f32),
+                pltpu.VMEM((2 * far, queries, own // 2), f32),
+                pltpu.VMEM((2 * far, queries, own // 2), f32),
                 pltpu.VMEM((group, 4, stat_lanes), f32),
                 pltpu.VMEM((group, rows, cols), f32),
                 pltpu.VMEM((group, rows, cols), f32),
-                pltpu.VMEM((widths, rows, cols), f32),
+                pltpu.VMEM((rows, cols), f32),
                 pltpu.VMEM((queries, own), bf16),
                 dma((7 + widths,)),
                 dma((blocks,)),
                 dma((blocks,)),
                 dma((blocks,)),
                 dma((blocks,)),
-                dma((outer,)),
-                dma((outer,)),
-                dma((far,)),
-                dma((far,)),
-                dma((group,)),
-                dma((group,)),
-                dma((group,)),
-                dma((group,)),
+                dma((2 * outer,)),
+                dma((2 * outer,)),
+                dma((2 * far,)),
+                dma((2 * far,)),
+                dma((1,)),
+                dma((1,)),
+                dma((1,)),
+                dma((1,)),
                 dma((widths,)),
                 dma((widths,)),
             ],
@@ -400,6 +433,9 @@
         grad_passage = s_scale * lax.dot_general(
             slope, queries_all.reshape(queries, s_width), TN, preferred_element_type=f32
         )
+        if not whole_tiles:
+            pieces = grad_query.reshape(outer, 2, rows, cols)
+            grad_query = pieces.transpose(1, 2, 0, 3).reshape(panel, s_width)
         return grad_query, grad_passage
 
     placed = (

time: 35.8 us -> 35.2 us (0.983)
  Pallas kernels: 31.9 us -> 31.3 us
    pallas_call x1, Pallas kernels: 31.9 us -> 31.3 us  [body(): pl.pallas_call(functools.partial(kernel, (blocks, widths, feats * widths,...]
where the time goes in v3:
time: 35.2 us; the launch traced here: 35.1 us
  Pallas kernels  31.3 us (89%)
  matrix products  2.47 us (7%)
  between operations  0.65 us (2%)
  local copies, waits for them, and re-layouts  0.62 us (2%)
    pallas_call x1, Pallas kernels, body(): pl.pallas_call(functools.partial(kernel, (blocks, widths, feats * widths,...  31.3 us
    dot_general x1, matrix products, body(): lax.dot_general(slope, queries_all.reshape(queries, s_width), TN, preferr...  2.47 us

profile of v3, /device:TPU:0, one launch (start us, length us, event | category | flops | bytes accessed | tf_op | source)
XLA Modules:
  0.0 35.1 jit_solution(1972016736305209053)
XLA Ops:
  0.6 31.3 %shard_map.77 = (f32[16,768]{1,0:T(8,128)}, bf16[64,512]{1,0:T(8,128)(2,1)}, bf16[4,16,768]{2,1,0:T(8,128)(2,1)}) custom-call(bf16[16,1024]{1,0:T(8,128)(2,1)} %tq_ref.1, bf16[2048,1024]{1,0:T(8,128)(2,1)} %tp_ref.1, bf16[16,768]{1,0:T(8,128)(2,1)} %sq_ref.1, bf16[512,768]{1,0:T(8,128)(2,1)} %sp_ref.1, s32[1,64]{1,0:T(1,128)} %bitcast.7, s32[64,128]{1,0:T(8,128)} %bitcast.6), custom_call_target="tpu_custom_call" | custom-call | tf_op jit(solution)/shard_map/pallas_call | solution.py:380
  32.0 0.0 copy-start
  32.0 2.5 %convolution_multiply_fusion = f32[512,768]{1,0:T(8,128)} fusion(bf16[64,512]{1,0:T(8,128)(2,1)} %get-tuple-element.6, bf16[64,768]{1,0:T(8,128)(2,1)} %bitcast.5), kind=kOutput, calls=%fused_computation | convolution fusion | flops 50724864 | bytes 1736704 | tf_op jit(solution)/shard_map/dot_general | solution.py:433
  34.4 0.0 copy-done
  34.4 0.6 %copy.9 = f32[16,768]{1,0:T(8,128)} copy(f32[16,768]{1,0:T(8,128)S(1)} %copy-done) | data formatting | bytes 98304
Async XLA Ops:
  32.0 2.5 %copy-start = (f32[16,768]{1,0:T(8,128)S(1)}, f32[16,768]{1,0:T(8,128)}, u32[]{:S(2)}) copy-start(f32[16,768]{1,0:T(8,128)} %get-tuple-element.10) | copy-start | bytes 147460

commit v4 on v3

--- a/solution.py
+++ b/solution.py
@@ -235,7 +235,7 @@
         highest = jnp.max(filled, axis=1, keepdims=True)
         powers = jnp.exp(filled - highest)
         summed = jnp.sum(powers, axis=1, keepdims=True)
-        return to_row(highest), to_row(summed)
+        return to_row(highest), to_row(summed), highest, powers
 
     sq_own.wait()
     for copy in sq_copies:
@@ -244,7 +244,7 @@
     queries_all = sq_all[...].reshape(queries, s_width)
     learn = lax.dot_general(queries_all, sp_v[...], NT, preferred_element_type=jnp.float32)
     learn_fill = jnp.where(masked, MASK_FILL, learn * s_scale)
-    learn_high, learn_sum = totals(learn_fill)
+    learn_high, learn_sum, learn_top, learn_powers = totals(learn_fill)
 
     teach = [finish(half, outer - 1) for half in range(2)]
     for place, copy in enumerate(far_copies):
@@ -252,7 +252,7 @@
         teach[place % 2] = teach[place % 2] + far_in[place]
     teach = jnp.concatenate(teach, axis=1)
     teach_fill = jnp.where(masked, MASK_FILL, teach * t_scale)
-    teach_high, teach_sum = totals(teach_fill)
+    teach_high, teach_sum, teach_top, teach_powers = totals(teach_fill)
 
     for i, value in enumerate((teach_high, learn_high, teach_sum, learn_sum)):
         stat[0, i : i + 1, :queries] = value
@@ -285,8 +285,8 @@
     logs = high + jnp.log(over(0, group, add_total, jnp.zeros((2, queries), jnp.float32)))
     teach_log = to_column(logs[0:1])
     learn_log = to_column(logs[1:2])
-    teach_probs = jnp.exp(teach_fill - teach_log)
-    learn_probs = jnp.exp(learn_fill - learn_log)
+    teach_probs = teach_powers * jnp.exp(teach_top - teach_log)
+    learn_probs = learn_powers * jnp.exp(learn_top - learn_log)
     slope = (2.0 * learn_probs - teach_probs - is_positive.astype(jnp.float32)).astype(
         jnp.bfloat16
     )

time: 35.2 us -> 35.2 us (level)
  no operation moved by 1% of the time
where the time goes in v4:
time: 35.2 us; the launch traced here: 35.1 us
  Pallas kernels  31.3 us (89%)
  matrix products  2.47 us (7%)
  between operations  0.65 us (2%)
  local copies, waits for them, and re-layouts  0.62 us (2%)
    pallas_call x1, Pallas kernels, body(): pl.pallas_call(functools.partial(kernel, (blocks, widths, feats * widths,...  31.3 us
    dot_general x1, matrix products, body(): lax.dot_general(slope, queries_all.reshape(queries, s_width), TN, preferr...  2.47 us

profile of v4, /device:TPU:0, one launch (start us, length us, event | category | flops | bytes accessed | tf_op | source)
XLA Modules:
  0.0 35.1 jit_solution(8886766402205925442)
XLA Ops:
  0.6 31.3 %shard_map.77 = (f32[16,768]{1,0:T(8,128)}, bf16[64,512]{1,0:T(8,128)(2,1)}, bf16[4,16,768]{2,1,0:T(8,128)(2,1)}) custom-call(bf16[16,1024]{1,0:T(8,128)(2,1)} %tq_ref.1, bf16[2048,1024]{1,0:T(8,128)(2,1)} %tp_ref.1, bf16[16,768]{1,0:T(8,128)(2,1)} %sq_ref.1, bf16[512,768]{1,0:T(8,128)(2,1)} %sp_ref.1, s32[1,64]{1,0:T(1,128)} %bitcast.7, s32[64,128]{1,0:T(8,128)} %bitcast.6), custom_call_target="tpu_custom_call" | custom-call | tf_op jit(solution)/shard_map/pallas_call | solution.py:380
  31.9 0.0 copy-start
  32.0 2.5 %convolution_multiply_fusion = f32[512,768]{1,0:T(8,128)} fusion(bf16[64,512]{1,0:T(8,128)(2,1)} %get-tuple-element.6, bf16[64,768]{1,0:T(8,128)(2,1)} %bitcast.5), kind=kOutput, calls=%fused_computation | convolution fusion | flops 50724864 | bytes 1736704 | tf_op jit(solution)/shard_map/dot_general | solution.py:433
  34.4 0.0 copy-done
  34.4 0.6 %copy.9 = f32[16,768]{1,0:T(8,128)} copy(f32[16,768]{1,0:T(8,128)S(1)} %copy-done) | data formatting | bytes 98304
Async XLA Ops:
  31.9 2.5 %copy-start = (f32[16,768]{1,0:T(8,128)S(1)}, f32[16,768]{1,0:T(8,128)}, u32[]{:S(2)}) copy-start(f32[16,768]{1,0:T(8,128)} %get-tuple-element.10) | copy-start | bytes 147460
